TPU v7x, 32 devices: a whole 2x2x4 slice. The times are simulated.
32 devices in a mesh: energy: 8 (over z, y), slab: 4 (over x, core).
Axes of the slice: x: 2, y: 2, z: 4, core: 2. Of those that a mesh axis runs over, the one named last changes fastest.
Arguments:
- energy_real: float32 [32], P('energy'), may hold values from -2 to 2
- energy_imag: float32 [32], P('energy'), may hold values from 1 to 2
- potential: float32 [4, 256], P('slab'), may hold values from -1.5 to 1.5
- onsite: float32 [4, 2, 256, 256], P('slab'), may hold values from -0.078125 to 0.078125
- coupling: float32 [4, 2, 256, 256], P('slab'), may hold values from -1.1 to 1.1
- deform: float32 [4, 256, 256], P('slab'), may hold values from 0.2 to 1
- offsets: int32 [8], replicated, may hold values from -8 to 8, as said below
- weights: int32 [8], replicated, may hold values from 8 to 40
Outputs:
- green: float32 [32, 4, 2, 256, 256], P('energy', 'slab')
- self_energy: float32 [32, 4, 2, 256, 256], P('energy', 'slab')
Inputs may be any that keep to these rules, and one draw needn't show every extreme that they name: Eight offsets; -8 and 8 are always among them.
All inputs are finite; a program needn't handle non-finite values.
Results may differ from a plain program's by a relative error of at most 0.0001.
Values sent between devices are 32-bit elements; how exact they have to be, the bound alone decides.
A program may use at most 128 MiB of HBM per device.

v0:
```python
import functools

import jax
import jax.numpy as jnp
from jax import lax
from jax.experimental import pallas as pl
from jax.experimental.pallas import tpu as pltpu
from jax.sharding import PartitionSpec as P

MESH = pl.DeviceIdType.MESH
CHUNKS = 8
AHEAD = 3
F32 = jnp.float32
BF16 = jnp.bfloat16


def split(value):
    high = value.astype(BF16)
    return high, (value - high.astype(F32)).astype(BF16)


def put_left(ref, real, imag):
    order = real.shape[0]
    real_high, real_low = split(real)
    imag_high, imag_low = split(imag)
    top = (-imag_high, -imag_high, -imag_low, real_high, real_high, real_low)
    bottom = (real_high, real_high, real_low, imag_high, imag_high, imag_low)
    for place in range(6):
        cut = slice(place * order, (place + 1) * order)
        ref[:order, cut] = top[place]
        ref[order:, cut] = bottom[place]


def put_right(ref, real, imag):
    order = real.shape[0]
    real_high, real_low = split(real)
    imag_high, imag_low = split(imag)
    parts = (imag_high, imag_low, imag_high, real_high, real_low, real_high)
    for place in range(6):
        ref[place * order : (place + 1) * order] = parts[place]


def product(left, right):
    both = jnp.dot(left[...], right[...], preferred_element_type=F32)
    order = right.shape[1]
    return both[:order], both[order:]


def kernel(
    n, slabs, er_ref, ei_ref, table_ref, potential_ref, onsite_ref, coupling_ref, deform_ref,
    green_ref, sigma_ref,
    base_ref, big, couple, c_left, c_right, left, right, pair, from_low, from_high, to_low, to_high,
    go, base_send, base_recv, slot_send, slot_recv, pair_send, pair_recv, low_send, low_recv, high_send, high_recv,
):
    energies = er_ref.shape[0]
    order = base_ref.shape[-1]
    rows = order // CHUNKS
    me = lax.axis_index("energy")
    q = lax.axis_index("slab")
    side = lax.rem(me, 2)
    partner = me + 1 - 2 * side
    has_low, has_high = me >= 2, me + 2 < n

    def at(energy, slab):
        return {"energy": energy, "slab": slab}

    barrier = pltpu.get_barrier_semaphore()

    def greet(present, energy, slab):
        @pl.when(present)
        def _():
            pl.semaphore_signal(barrier, inc=1, device_id=at(energy, slab), device_id_type=MESH)

    pl.semaphore_signal(barrier, inc=1, device_id=at(partner, q), device_id_type=MESH)
    greet(has_low, me - 2, q)
    greet(has_high, me + 2, q)
    greet(q >= 1, me, q - 1)
    greet(q + 1 < slabs, me, q + 1)

    identity_mask = lax.broadcasted_iota(jnp.int32, (order, order), 0) == lax.broadcasted_iota(
        jnp.int32, (order, order), 1
    )
    middle = max(slabs - 2, 1)
    base_ref[0, 0] = jnp.where(identity_mask, -potential_ref[...] - onsite_ref[0], -onsite_ref[0])
    base_ref[0, 1] = -onsite_ref[1]
    sigma_ref[...] = jnp.zeros_like(sigma_ref)
    put_left(c_left, coupling_ref[0], coupling_ref[1])
    put_right(c_right, coupling_ref[0].T, -coupling_ref[1].T)

    peers = 1
    for present in (has_low, has_high, q >= 1, q + 1 < slabs):
        peers = peers + jnp.where(present, 1, 0)
    pl.semaphore_wait(barrier, peers)

    base_copy = pltpu.make_async_remote_copy(
        src_ref=base_ref.at[0],
        dst_ref=base_ref.at[1],
        send_sem=base_send,
        recv_sem=base_recv,
        device_id=at(me, lax.rem(q + 1, slabs)),
        device_id_type=MESH,
    )

    @pl.when((q >= 1) & (q + 1 <= middle))
    def _():
        base_copy.start()

    @pl.when((q >= 2) & (q <= middle))
    def _():
        base_copy.wait_recv()

    def slot_copy(source, slot, energy):
        return pltpu.make_async_remote_copy(
            src_ref=big.at[source, energy],
            dst_ref=big.at[6 + slot, energy],
            send_sem=slot_send.at[slot, energy],
            recv_sem=slot_recv.at[slot, energy],
            device_id=at(me, lax.rem(q + 1, slabs)),
            device_id_type=MESH,
        )

    def compute(outer, sweep, energy):
        local = (outer == 0) & (sweep == 1) & (q >= 2)
        held = (outer == 1) & (sweep == 0)
        source = jnp.where(local, 0, 6 + outer * sweep)
        coupled = (q >= 1) & jnp.logical_not((outer == 0) & (sweep == 0))

        @pl.when(coupled & jnp.logical_not(local | held))
        def _():
            slot_copy(0, outer * sweep, energy).wait_recv()

        @pl.when(coupled)
        def _():
            put_right(right, big[source, energy, 0], big[source, energy, 1])
            put_left(left, *product(c_left, right))
            couple[0], couple[1] = product(left, c_right)

        @pl.when(jnp.logical_not(coupled))
        def _():
            couple[...] = jnp.zeros_like(couple)

        which = jnp.where((outer == 0) & (sweep == 0), 1, 0)
        ar = base_ref[which, 0] - sigma_ref[energy, 0, 0] - couple[0]
        ai = base_ref[which, 1] - sigma_ref[energy, 0, 1] - couple[1]
        dr = jnp.where(identity_mask, ar + er_ref[energy], 0.0)
        di = jnp.where(identity_mask, ai + ei_ref[energy], 0.0)

        def reciprocal(axis):
            r, i = jnp.sum(dr, axis=axis, keepdims=True), jnp.sum(di, axis=axis, keepdims=True)
            modulus = r * r + i * i
            return r / modulus, -i / modulus

        col_r, col_i = reciprocal(0)
        row_r, row_i = reciprocal(1)
        off_r = jnp.where(identity_mask, 0.0, ar)
        off_i = jnp.where(identity_mask, 0.0, ai)
        w_r = off_r * col_r - off_i * col_i
        w_i = off_r * col_i + off_i * col_r
        couple[0], couple[1] = w_r, w_i
        put_left(left, w_r, w_i)
        put_right(right, w_r, w_i)
        s_r, s_i = product(left, right)
        couple[0] = s_r - couple[0] + jnp.where(identity_mask, 1.0, 0.0)
        couple[1] = s_i - couple[1]
        put_right(right, s_r, s_i)
        p_r, p_i = product(left, right)
        y_r, y_i = couple[0] - p_r, couple[1] - p_i
        target = 3 * outer + sweep
        big[target, energy, 0] = row_r * y_r - row_i * y_i
        big[target, energy, 1] = row_r * y_i + row_i * y_r

        slot = jnp.where(outer == 0, 0, sweep + 1)
        first = (outer == 0) & (sweep == 1)
        second = (outer == 1) & (sweep == 0) & (q + 1 <= middle)
        third = (outer == 1) & (sweep == 1)

        @pl.when((q + 1 < slabs) & (first | second | third))
        def _():
            slot_copy(target, slot, energy).start()

    def pair_copy(outer, final, c):
        cut = pl.ds(c * rows, rows)
        return pltpu.make_async_remote_copy(
            src_ref=big.at[final, :, :, cut],
            dst_ref=pair.at[outer, :, :, cut],
            send_sem=pair_send.at[outer, c],
            recv_sem=pair_recv.at[outer, c],
            device_id=at(partner, q),
            device_id_type=MESH,
        )

    def low_copy(outer, c):
        cut = pl.ds(c * rows, rows)
        return pltpu.make_async_remote_copy(
            src_ref=to_low.at[:, :, cut],
            dst_ref=from_high.at[outer, :, :, cut],
            send_sem=low_send.at[outer, c],
            recv_sem=low_recv.at[outer, c],
            device_id=at(lax.rem(me + n - 2, n), q),
            device_id_type=MESH,
        )

    def high_copy(outer, c):
        cut = pl.ds(c * rows, rows)
        return pltpu.make_async_remote_copy(
            src_ref=to_high.at[:, :, cut],
            dst_ref=from_low.at[outer, :, :, cut],
            send_sem=high_send.at[outer, c],
            recv_sem=high_recv.at[outer, c],
            device_id=at(lax.rem(me + 2, n), q),
            device_id_type=MESH,
        )

    zero_at = 4 * energies - 1
    step_to_partner = energies * (1 - 2 * side)
    strip = 8

    def each_strip(c, body):
        def one(index, carry):
            body(pl.ds(pl.multiple_of(c * rows + index * strip, strip), strip))
            return carry

        lax.fori_loop(0, rows // strip, one, 0)

    def exchange(outer):
        final = jnp.where(outer == 0, jnp.where(q >= 2, 2, 1), 3 + jnp.minimum(q, 2))
        yields = (outer == 0) & (q == 0) & (slabs >= 2)

        def start_rest():
            for c in range(AHEAD, CHUNKS):
                pair_copy(outer, final, c).start()

        for c in range(AHEAD):
            pair_copy(outer, final, c).start()
        pl.when(jnp.logical_not(yields))(start_rest)
        for c in range(CHUNKS):
            if c == AHEAD:

                @pl.when(yields)
                def _():
                    pl.semaphore_wait(go, 1)
                    start_rest()

            pair_copy(outer, final, c).wait_recv()
            if c == CHUNKS - 2:

                @pl.when((outer == 0) & (q == 1))
                def _():
                    pl.semaphore_signal(go, inc=1, device_id=at(me, q - 1), device_id_type=MESH)

            def sums(shift, goal, final=final):
                weight = [
                    [
                        [
                            table_ref[zero_at + shift + b - a + extra]
                            for extra in (0, step_to_partner)
                        ]
                        for b in range(energies)
                    ]
                    for a in range(energies)
                ]

                def body(cut):
                    for part in range(2):
                        own = [big[final, b, part, cut] for b in range(energies)]
                        other = [pair[outer, b, part, cut] for b in range(energies)]
                        for a in range(energies):
                            total = weight[a][0][0] * own[0]
                            for b in range(energies):
                                if b:
                                    total = total + weight[a][b][0] * own[b]
                                total = total + weight[a][b][1] * other[b]
                            goal(a, part, cut, total)

                each_strip(c, body)

            def put_high(a, part, cut, value):
                to_high[a, part, cut] = value

            def put_low(a, part, cut, value):
                to_low[a, part, cut] = value

            def put_own(a, part, cut, value):
                sigma_ref[a, 0, part, cut] = value

            @pl.when(has_high)
            def _():
                sums(-2 * energies, put_high)
                high_copy(outer, c).start()

            @pl.when(has_low)
            def _():
                sums(2 * energies, put_low)
                low_copy(outer, c).start()

            sums(0, put_own)

        for c in range(CHUNKS):

            def add(source):
                def body(cut):
                    for a in range(energies):
                        for part in range(2):
                            sigma_ref[a, 0, part, cut] += source[outer, a, part, cut]

                each_strip(c, body)

            @pl.when(has_low)
            def _():
                high_copy(outer, c).wait_recv()
                add(from_low)

            @pl.when(has_high)
            def _():
                low_copy(outer, c).wait_recv()
                add(from_high)

            def scale(cut):
                level = deform_ref[cut]
                for a in range(energies):
                    for part in range(2):
                        sigma_ref[a, 0, part, cut] = level * sigma_ref[a, 0, part, cut]

            each_strip(c, scale)

        for c in range(CHUNKS):
            pair_copy(outer, final, c).wait_send()

            @pl.when(has_high)
            def _():
                high_copy(outer, c).wait_send()

            @pl.when(has_low)
            def _():
                low_copy(outer, c).wait_send()

    def outer_step(outer, carry):
        def step(j, inner):
            paired = (outer == 0) & (j < 2 * energies)
            sweep = jnp.where(paired, lax.rem(j, 2), lax.div(j, energies))
            energy = jnp.where(paired, lax.div(j, 2), lax.rem(j, energies))
            start = ((outer == 0) & (q >= 2) & (q <= middle)) | ((outer == 1) & (q <= 1))
            mid = (q <= middle) & ((outer == 0) | (q >= 1))
            active = (
                ((sweep == 0) & start) | ((sweep == 1) & mid) | ((sweep == 2) & (q >= 2))
            )

            @pl.when(active)
            def _():
                compute(outer, sweep, energy)

            return inner

        lax.fori_loop(0, 3 * energies, step, 0)
        exchange(outer)
        return carry

    lax.fori_loop(0, 2, outer_step, 0)

    final = 3 + jnp.minimum(q, 2)

    def out(index, carry):
        cut = pl.ds(pl.multiple_of(index * 64, 64), 64)
        for a in range(energies):
            for part in range(2):
                green_ref[a, 0, part, cut] = big[final, a, part, cut]
        return carry

    lax.fori_loop(0, order // 64, out, 0)

    def drain(slot, present):
        @pl.when(present & (q + 1 < slabs))
        def _():
            for energy in range(energies):
                slot_copy(0, slot, energy).wait_send()

    drain(0, q <= middle)
    drain(1, q + 1 <= middle)
    drain(2, (q >= 1) & (q <= middle))

    @pl.when((q >= 1) & (q + 1 <= middle))
    def _():
        base_copy.wait_send()


def on_device(n, slabs, energy_real, energy_imag, potential, onsite, coupling, deform, offsets, weights):
    order = onsite.shape[-1]
    energies = energy_real.shape[0]
    gap = jnp.arange(8 * energies - 1, dtype=jnp.int32) - (4 * energies - 1)
    table = jnp.sum(
        jnp.where(gap[:, None] == offsets[None, :], weights.astype(F32)[None, :] / 128.0, 0.0), axis=-1
    )
    shape = (energies, 1, 2, order, order)
    smem = pl.BlockSpec(memory_space=pltpu.SMEM)
    vmem = pl.BlockSpec(memory_space=pltpu.VMEM)
    block = (energies, 2, order, order)
    dma = pltpu.SemaphoreType.DMA
    return pl.pallas_call(
        functools.partial(kernel, n, slabs),
        out_shape=[jax.ShapeDtypeStruct(shape, F32)] * 2,
        in_specs=[smem, smem, smem, vmem, vmem, vmem, vmem],
        out_specs=[vmem, vmem],
        scratch_shapes=[
            pltpu.VMEM((2, 2, order, order), F32),
            pltpu.VMEM((9,) + block, F32),
            pltpu.VMEM((2, order, order), F32),
            pltpu.VMEM((2 * order, 6 * order), BF16),
            pltpu.VMEM((6 * order, order), BF16),
            pltpu.VMEM((2 * order, 6 * order), BF16),
            pltpu.VMEM((6 * order, order), BF16),
            pltpu.VMEM((2,) + block, F32),
            pltpu.VMEM((2,) + block, F32),
            pltpu.VMEM((2,) + block, F32),
            pltpu.VMEM(block, F32),
            pltpu.VMEM(block, F32),
            pltpu.SemaphoreType.REGULAR,
            dma,
            dma,
            dma((3, energies)),
            dma((3, energies)),
            dma((2, CHUNKS)),
            dma((2, CHUNKS)),
            dma((2, CHUNKS)),
            dma((2, CHUNKS)),
            dma((2, CHUNKS)),
            dma((2, CHUNKS)),
        ],
        compiler_params=pltpu.CompilerParams(
            collective_id=0, has_side_effects=True, vmem_limit_bytes=60 * 2**20
        ),
    )(energy_real, energy_imag, table, potential, onsite[0], coupling[0], deform[0])


def solution(mesh):
    return jax.shard_map(
        functools.partial(on_device, mesh.shape["energy"], mesh.shape["slab"]),
        mesh=mesh,
        in_specs=(
            P("energy"),
            P("energy"),
            P("slab", None),
            P("slab", None, None, None),
            P("slab", None, None, None),
            P("slab", None, None),
            P(),
            P(),
        ),
        out_specs=(P("energy", "slab", None, None, None), P("energy", "slab", None, None, None)),
        check_vma=False,
    )
```

profile of v0, /device:TPU:2, one launch (start us, length us, event | category | flops | bytes accessed | tf_op | source)
XLA Modules:
  0.0 182.9 jit_solution(5334154096016433569)
XLA Ops:
  0.6 0.7 convert_multiply_fusion
  1.3 1.2 select_reduce_fusion.table_ref
  2.5 175.8 %shard_map.95 = (f32[4,1,2,256,256]{4,3,2,1,0:T(8,128)}, f32[4,1,2,256,256]{4,3,2,1,0:T(8,128)}) custom-call(f32[4]{0:T(128)} %er_ref.1, f32[4]{0:T(128)} %ei_ref.1, f32[31]{0:T(128)} %select_reduce_fusion.table_ref, f32[1,256]{1,0:T(1,128)} %potential_ref.1, f32[2,256,256]{2,1,0:T(8,128)} %bitcast.3, f32[2,256,256]{2,1,0:T(8,128)} %bitcast.4, ...), custom_call_target="tpu_custom_call" | custom-call | tf_op jit(solution)/shard_map/pallas_call | solution.py:398
  178.3 0.0 copy-start
  178.3 3.2 %copy.12 = f32[4,1,2,256,256]{4,3,2,1,0:T(8,128)} copy(f32[4,1,2,256,256]{4,3,2,1,0:T(8,128)} %get-tuple-element.4) | data formatting | bytes 4194304
  181.5 0.0 copy-done
  181.5 1.3 copy.13
  (1 shorter events, 0.0 us)
Async XLA Ops:
  178.3 3.2 %copy-start = (f32[4,1,2,256,256]{4,3,2,1,0:T(8,128)S(1)}, f32[4,1,2,256,256]{4,3,2,1,0:T(8,128)}, u32[]{:S(2)}) copy-start(f32[4,1,2,256,256]{4,3,2,1,0:T(8,128)} %get-tuple-element.5) | copy-start | bytes 6291460
where the time goes:
time: 183 us
  Pallas kernels  176 us (96%)
  local copies, waits for them, and re-layouts  4.52 us (2%)
  other arithmetic  1.91 us (1%)
    pallas_call x1, Pallas kernels, on_device(): pl.pallas_call(functools.partial(kernel, n, slabs), out_shape=[jax.ShapeD...  176 us
    unnamed x4, local copies, waits for them, and re-layouts  4.52 us

commit v1 on v0

--- a/solution.py
+++ b/solution.py
@@ -23,27 +23,27 @@
     order = real.shape[0]
     real_high, real_low = split(real)
     imag_high, imag_low = split(imag)
-    top = (-imag_high, -imag_high, -imag_low, real_high, real_high, real_low)
-    bottom = (real_high, real_high, real_low, imag_high, imag_high, imag_low)
+    parts = (real_high, real_high, real_low, imag_high, imag_high, imag_low)
     for place in range(6):
-        cut = slice(place * order, (place + 1) * order)
-        ref[:order, cut] = top[place]
-        ref[order:, cut] = bottom[place]
+        ref[:, place * order : (place + 1) * order] = parts[place]
 
 
 def put_right(ref, real, imag):
     order = real.shape[0]
     real_high, real_low = split(real)
     imag_high, imag_low = split(imag)
-    parts = (imag_high, imag_low, imag_high, real_high, real_low, real_high)
+    first = (real_high, real_low, real_high, -imag_high, -imag_low, -imag_high)
+    second = (imag_high, imag_low, imag_high, real_high, real_low, real_high)
     for place in range(6):
-        ref[place * order : (place + 1) * order] = parts[place]
+        cut = slice(place * order, (place + 1) * order)
+        ref[cut, :order] = first[place]
+        ref[cut, order:] = second[place]
 
 
 def product(left, right):
     both = jnp.dot(left[...], right[...], preferred_element_type=F32)
-    order = right.shape[1]
-    return both[:order], both[order:]
+    order = left.shape[0]
+    return both[:, :order], both[:, order:]
 
 
 def kernel(
@@ -404,10 +404,10 @@
             pltpu.VMEM((2, 2, order, order), F32),
             pltpu.VMEM((9,) + block, F32),
             pltpu.VMEM((2, order, order), F32),
-            pltpu.VMEM((2 * order, 6 * order), BF16),
-            pltpu.VMEM((6 * order, order), BF16),
-            pltpu.VMEM((2 * order, 6 * order), BF16),
-            pltpu.VMEM((6 * order, order), BF16),
+            pltpu.VMEM((order, 6 * order), BF16),
+            pltpu.VMEM((6 * order, 2 * order), BF16),
+            pltpu.VMEM((order, 6 * order), BF16),
+            pltpu.VMEM((6 * order, 2 * order), BF16),
             pltpu.VMEM((2,) + block, F32),
             pltpu.VMEM((2,) + block, F32),
             pltpu.VMEM((2,) + block, F32),

time: 183 us -> 164 us (0.90)
  Pallas kernels: 176 us -> 157 us
    pallas_call x1, Pallas kernels: 176 us -> 157 us  [on_device(): pl.pallas_call(functools.partial(kernel, n, slabs), out_shape=[jax.ShapeD...]
where the time goes in v1:
time: 164 us
  Pallas kernels  157 us (96%)
  local copies, waits for them, and re-layouts  4.52 us (3%)
  other arithmetic  1.91 us (1%)
    pallas_call x1, Pallas kernels, on_device(): pl.pallas_call(functools.partial(kernel, n, slabs), out_shape=[jax.ShapeD...  157 us
    unnamed x4, local copies, waits for them, and re-layouts  4.52 us

profile of v1, /device:TPU:2, one launch (start us, length us, event | category | flops | bytes accessed | tf_op | source)
XLA Modules:
  0.0 164.2 jit_solution(2781219273951675503)
XLA Ops:
  0.6 0.7 convert_multiply_fusion
  1.3 1.2 select_reduce_fusion.table_ref
  2.5 157.1 %shard_map.95 = (f32[4,1,2,256,256]{4,3,2,1,0:T(8,128)}, f32[4,1,2,256,256]{4,3,2,1,0:T(8,128)}) custom-call(f32[4]{0:T(128)} %er_ref.1, f32[4]{0:T(128)} %ei_ref.1, f32[31]{0:T(128)} %select_reduce_fusion.table_ref, f32[1,256]{1,0:T(1,128)} %potential_ref.1, f32[2,256,256]{2,1,0:T(8,128)} %bitcast.3, f32[2,256,256]{2,1,0:T(8,128)} %bitcast.4, ...), custom_call_target="tpu_custom_call" | custom-call | tf_op jit(solution)/shard_map/pallas_call | solution.py:398
  159.7 0.0 copy-start
  159.7 3.2 %copy.12 = f32[4,1,2,256,256]{4,3,2,1,0:T(8,128)} copy(f32[4,1,2,256,256]{4,3,2,1,0:T(8,128)} %get-tuple-element.4) | data formatting | bytes 4194304
  162.9 0.0 copy-done
  162.9 1.3 copy.13
  (1 shorter events, 0.0 us)
Async XLA Ops:
  159.7 3.2 %copy-start = (f32[4,1,2,256,256]{4,3,2,1,0:T(8,128)S(1)}, f32[4,1,2,256,256]{4,3,2,1,0:T(8,128)}, u32[]{:S(2)}) copy-start(f32[4,1,2,256,256]{4,3,2,1,0:T(8,128)} %get-tuple-element.5) | copy-start | bytes 6291460

commit v2 on v1

--- a/solution.py
+++ b/solution.py
@@ -9,7 +9,6 @@
 
 MESH = pl.DeviceIdType.MESH
 CHUNKS = 8
-AHEAD = 3
 F32 = jnp.float32
 BF16 = jnp.bfloat16
 
@@ -49,8 +48,8 @@
 def kernel(
     n, slabs, er_ref, ei_ref, table_ref, potential_ref, onsite_ref, coupling_ref, deform_ref,
     green_ref, sigma_ref,
-    base_ref, big, couple, c_left, c_right, left, right, pair, from_low, from_high, to_low, to_high,
-    go, base_send, base_recv, slot_send, slot_recv, pair_send, pair_recv, low_send, low_recv, high_send, high_recv,
+    base_ref, big, kept, couple, c_left, c_right, left, right, pair, from_low, from_high, to_low, to_high,
+    base_send, base_recv, slot_send, slot_recv, pair_send, pair_recv, low_send, low_recv, high_send, high_recv,
 ):
     energies = er_ref.shape[0]
     order = base_ref.shape[-1]
@@ -129,11 +128,19 @@
         def _():
             slot_copy(0, outer * sweep, energy).wait_recv()
 
-        @pl.when(coupled)
+        @pl.when(coupled & held)
+        def _():
+            couple[...] = kept[energy]
+
+        @pl.when(coupled & jnp.logical_not(held))
         def _():
             put_right(right, big[source, energy, 0], big[source, energy, 1])
             put_left(left, *product(c_left, right))
             couple[0], couple[1] = product(left, c_right)
+
+        @pl.when(coupled & (outer == 0) & (sweep == 1))
+        def _():
+            kept[energy] = couple[...]
 
         @pl.when(jnp.logical_not(coupled))
         def _():
@@ -224,29 +231,10 @@
 
     def exchange(outer):
         final = jnp.where(outer == 0, jnp.where(q >= 2, 2, 1), 3 + jnp.minimum(q, 2))
-        yields = (outer == 0) & (q == 0) & (slabs >= 2)
-
-        def start_rest():
-            for c in range(AHEAD, CHUNKS):
-                pair_copy(outer, final, c).start()
-
-        for c in range(AHEAD):
+        for c in range(CHUNKS):
             pair_copy(outer, final, c).start()
-        pl.when(jnp.logical_not(yields))(start_rest)
         for c in range(CHUNKS):
-            if c == AHEAD:
-
-                @pl.when(yields)
-                def _():
-                    pl.semaphore_wait(go, 1)
-                    start_rest()
-
             pair_copy(outer, final, c).wait_recv()
-            if c == CHUNKS - 2:
-
-                @pl.when((outer == 0) & (q == 1))
-                def _():
-                    pl.semaphore_signal(go, inc=1, device_id=at(me, q - 1), device_id_type=MESH)
 
             def sums(shift, goal, final=final):
                 weight = [
@@ -403,6 +391,7 @@
         scratch_shapes=[
             pltpu.VMEM((2, 2, order, order), F32),
             pltpu.VMEM((9,) + block, F32),
+            pltpu.VMEM(block, F32),
             pltpu.VMEM((2, order, order), F32),
             pltpu.VMEM((order, 6 * order), BF16),
             pltpu.VMEM((6 * order, 2 * order), BF16),
@@ -413,7 +402,6 @@
             pltpu.VMEM((2,) + block, F32),
             pltpu.VMEM(block, F32),
             pltpu.VMEM(block, F32),
-            pltpu.SemaphoreType.REGULAR,
             dma,
             dma,
             dma((3, energies)),

time: 164 us -> 165 us (level)
  no operation moved by 1% of the time
where the time goes in v2:
time: 165 us; the launch traced here: 164 us
  Pallas kernels  157 us (95%)
  local copies, waits for them, and re-layouts  4.52 us (3%)
  other arithmetic  1.91 us (1%)
    pallas_call x1, Pallas kernels, on_device(): pl.pallas_call(functools.partial(kernel, n, slabs), out_shape=[jax.ShapeD...  157 us
    unnamed x4, local copies, waits for them, and re-layouts  4.52 us

profile of v2, /device:TPU:2, one launch (start us, length us, event | category | flops | bytes accessed | tf_op | source)
XLA Modules:
  0.0 164.3 jit_solution(6651750550499294285)
XLA Ops:
  0.6 0.7 convert_multiply_fusion
  1.3 1.2 select_reduce_fusion.table_ref
  2.5 157.3 %shard_map.95 = (f32[4,1,2,256,256]{4,3,2,1,0:T(8,128)}, f32[4,1,2,256,256]{4,3,2,1,0:T(8,128)}) custom-call(f32[4]{0:T(128)} %er_ref.1, f32[4]{0:T(128)} %ei_ref.1, f32[31]{0:T(128)} %select_reduce_fusion.table_ref, f32[1,256]{1,0:T(1,128)} %potential_ref.1, f32[2,256,256]{2,1,0:T(8,128)} %bitcast.3, f32[2,256,256]{2,1,0:T(8,128)} %bitcast.4, ...), custom_call_target="tpu_custom_call" | custom-call | tf_op jit(solution)/shard_map/pallas_call | solution.py:386
  159.8 0.0 copy-start
  159.8 3.2 %copy.12 = f32[4,1,2,256,256]{4,3,2,1,0:T(8,128)} copy(f32[4,1,2,256,256]{4,3,2,1,0:T(8,128)} %get-tuple-element.4) | data formatting | bytes 4194304
  163.0 0.0 copy-done
  163.0 1.3 copy.13
  (1 shorter events, 0.0 us)
Async XLA Ops:
  159.8 3.2 %copy-start = (f32[4,1,2,256,256]{4,3,2,1,0:T(8,128)S(1)}, f32[4,1,2,256,256]{4,3,2,1,0:T(8,128)}, u32[]{:S(2)}) copy-start(f32[4,1,2,256,256]{4,3,2,1,0:T(8,128)} %get-tuple-element.5) | copy-start | bytes 6291460
